TPU v7x, 256 devices: a whole 4x4x8 slice. The times are simulated.
256 devices in a mesh: chan: 64 (over z, x, y_lo), tm: 4 (over y_hi, core).
Axes of the slice: x: 4, y: 4 (y_hi: 2, y_lo: 2; y = y_hi * 2 + y_lo), z: 8, core: 2. Of those that a mesh axis runs over, the one named last changes fastest.
Arguments:
- traces: bfloat16 [128, 1024, 3000], P('tm', 'chan'), may hold values from -6 to 6
- valid: int32 [128, 1024], P('tm', 'chan'), may hold values 0 or 1
- sources: int32 [512], replicated, may hold values from 0 to 1023, as said below
Outputs:
- cross: bfloat16 [2, 1024, 512, 1024], P(None, ('chan', 'tm'))
Inputs may be any that keep to these rules, and one draw needn't show every extreme that they name: `sources`: distinct channel indices; channels 0 and 1023 are always among them.
All inputs are finite; a program needn't handle non-finite values. No bound on the sum of `valid` on one device may be relied on, other than what follows from the above.
Results may differ from a plain program's by a relative error of at most 0.0066.
Values may be sent and summed in bfloat16 or wider, within the bound.
A program may use at most 128 MiB of HBM per device.

v0:
```python
import math

import jax
import jax.numpy as jnp
from jax import lax
from jax.sharding import PartitionSpec as P

F = 1024
LOW_BIN = 6
HALF_SPAN = 32


def dft_tables(count, samples):
    times = jnp.arange(samples, dtype=jnp.int32)
    bins = LOW_BIN + jnp.arange(count, dtype=jnp.int32)
    phase = times[:, None] * bins[None, :] % samples
    angle = 2.0 * math.pi / samples * phase.astype(jnp.float32)
    taper = 0.5 - 0.5 * jnp.cos(2.0 * math.pi / samples * times.astype(jnp.float32))
    cosine = (taper[:, None] * jnp.cos(angle)).astype(jnp.bfloat16)
    sine = (taper[:, None] * jnp.sin(angle)).astype(jnp.bfloat16)
    return jnp.concatenate([cosine, sine], axis=1)


def band_ones(nbins):
    index = jnp.arange(nbins, dtype=jnp.int32)
    inside = (jnp.abs(index[:, None] - index[None, :]) <= HALF_SPAN).astype(jnp.float32)
    return (inside.astype(jnp.bfloat16), jnp.sum(inside, axis=0))


def body(traces, valid, sources):
    win_dev, ch_dev, samples = traces.shape
    sample_rows = traces.reshape(win_dev * ch_dev, samples)
    table = dft_tables(F, samples)
    both = jnp.dot(sample_rows, table, preferred_element_type=jnp.float32)
    real_part = both[:, :F]
    imag_part = -both[:, F:]
    amplitude = jnp.sqrt(real_part * real_part + imag_part * imag_part).astype(jnp.bfloat16)
    ones_band, counts = band_ones(F)
    smooth = jnp.dot(amplitude, ones_band, preferred_element_type=jnp.float32) / counts[None, :]
    scale = valid.reshape(win_dev * ch_dev, 1).astype(jnp.float32) / (smooth + 1e-06)
    white_re = (real_part * scale).astype(jnp.bfloat16).reshape(win_dev, ch_dev, F)
    white_im = (imag_part * scale).astype(jnp.bfloat16).reshape(win_dev, ch_dev, F)
    white = jnp.transpose(jnp.stack([white_re, white_im], axis=1), (0, 1, 3, 2))
    owned = lax.all_to_all(white, "chan", split_axis=2, concat_axis=3, tiled=True)
    regrouped = lax.all_to_all(owned, "tm", split_axis=2, concat_axis=0, tiled=True)
    chosen = jnp.take(regrouped, sources, axis=3)
    s_re = chosen[:, 0]
    s_im = chosen[:, 1]
    c_re = regrouped[:, 0]
    c_im = regrouped[:, 1]
    cross_re = jnp.einsum(
        "wfs,wfc->fsc", s_re, c_re, preferred_element_type=jnp.float32
    ) + jnp.einsum("wfs,wfc->fsc", s_im, c_im, preferred_element_type=jnp.float32)
    cross_im = jnp.einsum(
        "wfs,wfc->fsc", s_re, c_im, preferred_element_type=jnp.float32
    ) - jnp.einsum("wfs,wfc->fsc", s_im, c_re, preferred_element_type=jnp.float32)
    return jnp.stack([cross_re, cross_im], axis=0).astype(jnp.bfloat16)


def solution(mesh):
    placed = (P("tm", "chan", None), P("tm", "chan"), P())
    return jax.shard_map(
        body,
        mesh=mesh,
        in_specs=placed,
        out_specs=P(None, ("chan", "tm"), None, None),
        check_vma=False,
    )
```

profile of v0, /device:TPU:1, one launch (start us, length us, event | category | flops | bytes accessed | tf_op | source)
XLA Modules:
  0.0 251.7 jit_solution(18172833129993618383)
XLA Ops:
  0.0 0.0 copy-start
  0.0 0.2 convert_reduce_fusion
  0.2 0.1 multiply_subtract_fusion
  0.3 0.9 convert_element_type.53
  1.1 0.1 copy.27
  1.2 0.1 convert_element_type.54
  1.3 52.7 %multiply_convert_fusion.1 = (bf16[3000,1024]{1,0:T(8,128)(2,1)S(1)}, bf16[3000,1024]{1,0:T(8,128)(2,1)}) fusion(s32[1024]{0:T(1024)S(1)} %iota_add_fusion, f32[3000]{0:T(1024)S(1)} %multiply_subtract_fusion), kind=kLoop, calls=%fused_computation.9 | loop fusion | flops 39936000 | bytes 12304096 | tf_op jit(solution)/shard_map/convert_element_type | solution.py:19
  54.0 0.0 copy-done
  54.0 8.4 %fusion.11 = f32[512,2048]{1,0:T(8,128)} fusion(bf16[512,3000]{1,0:T(8,128)(2,1)S(1)} %bitcast.43, bf16[3000,1024]{1,0:T(8,128)(2,1)} %get-tuple-element.8, bf16[3000,1024]{1,0:T(8,128)(2,1)S(1)} %get-tuple-element.7), kind=kOutput, calls=%fused_computation.23 | convolution fusion | flops 6316032000 | bytes 19554304 | tf_op jit(solution)/shard_map/dot_general | solution.py:34
  62.4 5.2 %multiply_convert_fusion.3 = (bf16[512,1024]{1,0:T(8,128)(2,1)S(1)}, bf16[512,1024]{1,0:T(8,128)(2,1)S(1)}) fusion(f32[512,2048]{1,0:T(8,128)} %fusion.11, f32[1024]{0:T(1024)S(1)} %convert_reduce_fusion, f32[512]{0:T(512)S(1)} %convert_element_type.54), kind=kOutput, calls=%fused_computation.26 | convolution fusion | flops 1085276160 | bytes 10491904 | tf_op jit(solution)/shard_map/dot_general | solution.py:39
  67.6 5.1 %copy.29 = bf16[32,1,16,1024]{0,2,1,3:T(8,128)(2,1)} copy(bf16[32,1,16,1024]{3,2,0,1:T(8,128)(2,1)S(1)} %bitcast.53) | data formatting | bytes 2097152 | tf_op jit(solution)/shard_map/stack;reshape | solution.py:43
  72.7 5.1 %copy.28 = bf16[32,1,16,1024]{0,2,1,3:T(8,128)(2,1)} copy(bf16[32,1,16,1024]{3,2,0,1:T(8,128)(2,1)S(1)} %bitcast.52) | data formatting | bytes 2097152 | tf_op jit(solution)/shard_map/stack;reshape | solution.py:43
  77.8 8.5 %fusion.21 = bf16[1024,2,16,32]{3,2,1,0:T(8,128)(2,1)} fusion(bf16[32,1,16,1024]{0,2,1,3:T(8,128)(2,1)} %copy.29, bf16[32,1,16,1024]{0,2,1,3:T(8,128)(2,1)} %copy.28), kind=kLoop, calls=%fused_computation.45 | loop fusion | flops 1048576 | bytes 4194304
  86.3 12.2 %reshape.40 = bf16[64,2,8192]{2,1,0:T(2,128)(2,1)S(1)} reshape(bf16[1024,2,16,32]{3,2,1,0:T(8,128)(2,1)} %fusion.21) | data formatting | bytes 4194304
  98.5 61.6 %all_to_all.36 = bf16[64,2,8192]{2,1,0:T(2,128)(2,1)} all-to-all(bf16[64,2,8192]{2,1,0:T(2,128)(2,1)S(1)} %reshape.40), channel_id=1, replica_groups=mesh['chan'=64,'tm'=4] {'chan'}, dimensions={0} | all-to-all | bytes 4194304 | tf_op jit(solution)/shard_map/all_to_all | solution.py:44
  160.1 11.7 %reshape.41 = bf16[1024,2,16,32]{3,2,1,0:T(8,128)(2,1)} reshape(bf16[64,2,8192]{2,1,0:T(2,128)(2,1)} %all_to_all.36) | data formatting | bytes 4194304
  171.8 9.0 %copy.31 = bf16[32,2,16,64,16]{0,4,3,2,1:T(8,128)(2,1)} copy(bf16[32,2,16,64,16]{0,4,1,2,3:T(8,128)(2,1)} %bitcast.49) | data formatting | bytes 4194304 | tf_op jit(solution)/shard_map/all_to_all | solution.py:44
  180.8 8.0 %copy.32 = bf16[32,2,16,1024]{3,0,1,2:T(8,128)(2,1)} copy(bf16[32,2,16,1024]{0,3,2,1:T(8,128)(2,1)} %bitcast.50) | data formatting | bytes 4194304 | tf_op jit(solution)/shard_map/all_to_all | solution.py:44
  188.8 8.3 %all-to-all-start.1 = ((bf16[32,2,16,1024]{3,0,1,2:T(8,128)(2,1)}), bf16[32,2,16,1024]{3,0,1,2:T(8,128)(2,1)S(1)}, u32[]{:S(2)}, u32[]{:S(2)}) async-start(bf16[32,2,16,1024]{3,0,1,2:T(8,128)(2,1)} %copy.32), calls=%async_computation.1 | async-start | bytes 4194304 | tf_op jit(solution)/shard_map/all_to_all | solution.py:45
  197.0 0.0 copy-done.3
  197.1 26.3 %all-to-all-done.1 = bf16[32,2,16,1024]{3,0,1,2:T(8,128)(2,1)S(1)} async-done(((bf16[32,2,16,1024]{3,0,1,2:T(8,128)(2,1)}), bf16[32,2,16,1024]{3,0,1,2:T(8,128)(2,1)S(1)}, u32[]{:S(2)}, u32[]{:S(2)}) %all-to-all-start.1) | async-done | bytes 2097184 | tf_op jit(solution)/shard_map/all_to_all | solution.py:45
  223.4 1.3 copy-done.2
  224.7 1.9 copy.34
  226.6 2.5 %copy.35 = bf16[128,2,4,1024]{0,2,3,1:T(4,128)(2,1)} copy(bf16[128,2,4,1024]{3,0,2,1:T(8,128)(2,1)S(1)} %bitcast.44) | data formatting | bytes 4194304 | tf_op jit(solution)/shard_map/all_to_all | solution.py:45
  229.1 4.5 %gather_fusion = bf16[512,128,2,4]{1,3,2,0:T(4,128)(2,1)} fusion(bf16[128,2,4,1024]{0,2,3,1:T(4,128)(2,1)} %copy.35, s32[1024]{0:T(1024)S(1)} %pad_clamp_fusion), kind=kCustom, calls=%fused_computation | custom fusion | bytes 2099200 | tf_op jit(solution)/shard_map/jit(_take)/gather | solution.py:46
  233.6 1.4 fusion.16
  235.0 1.2 fusion.18
  236.2 1.2 fusion.17
  237.5 3.2 %fusion.10 = bf16[1,4,512,1024]{3,2,1,0:T(8,128)(2,1)} fusion(f32[4,512,1024]{2,1,0:T(8,128)S(1)} %fusion.18, bf16[128,2,4,1024]{3,0,2,1:T(8,128)(2,1)S(1)} %bitcast.47, bf16[128,2,4,512]{0,3,2,1:T(8,128)(2,1)S(1)} %fusion.16), kind=kOutput, calls=%fused_computation.21 | convolution fusion | flops 541065216 | bytes 14155776 | tf_op jit(solution)/shard_map/wfs,wfc->fsc/dot_general | solution.py:56
  240.7 3.3 %fusion.9 = bf16[1,4,512,1024]{3,2,1,0:T(8,128)(2,1)} fusion(f32[4,512,1024]{2,1,0:T(8,128)S(1)} %fusion.17, bf16[128,2,4,1024]{3,0,2,1:T(8,128)(2,1)S(1)} %bitcast.48, bf16[128,2,4,512]{0,3,2,1:T(8,128)(2,1)S(1)} %fusion.16), kind=kOutput, calls=%fused_computation.20 | convolution fusion | flops 541065216 | bytes 14155776 | tf_op jit(solution)/shard_map/wfs,wfc->fsc/dot_general | solution.py:53
  243.9 7.8 %pad_maximum_fusion = bf16[2,4,512,1024]{3,2,1,0:T(8,128)(2,1)} fusion(bf16[1,4,512,1024]{3,2,1,0:T(8,128)(2,1)} %fusion.10, bf16[1,4,512,1024]{3,2,1,0:T(8,128)(2,1)} %fusion.9), kind=kLoop, calls=%fused_computation.15 | loop fusion | flops 4194304 | bytes 16777216 | tf_op jit(solution)/shard_map/stack | solution.py:57
  251.7 0.0 copy-done.1
  (7 shorter events, 0.0 us)
Async XLA Ops:
  0.0 54.0 %copy-start = (bf16[32,16,3000]{2,1,0:T(8,128)(2,1)S(1)}, bf16[32,16,3000]{2,1,0:T(8,128)(2,1)}, u32[]{:S(2)}) copy-start(bf16[32,16,3000]{2,1,0:T(8,128)(2,1)} %param.3) | copy-start | bytes 9216004
  188.8 8.3 %copy-start.3 = (s32[512]{0:T(512)S(1)}, s32[512]{0:T(512)}, u32[]{:S(2)}) copy-start(s32[512]{0:T(512)} %param.5) | copy-start | bytes 6148
  188.8 34.6 %all-to-all-start.1 = ((bf16[32,2,16,1024]{3,0,1,2:T(8,128)(2,1)}), bf16[32,2,16,1024]{3,0,1,2:T(8,128)(2,1)S(1)}, u32[]{:S(2)}, u32[]{:S(2)}) async-start(bf16[32,2,16,1024]{3,0,1,2:T(8,128)(2,1)} %copy.32), calls=%async_computation.1 | async-start | bytes 4194304 | tf_op jit(solution)/shard_map/all_to_all | solution.py:45
  223.4 1.3 copy-start.2
  243.9 7.8 %copy-start.1 = (bf16[32,16,3000]{2,1,0:T(8,128)(2,1)S(1)}, bf16[32,16,3000]{2,1,0:T(8,128)(2,1)}, u32[]{:S(2)}) copy-start(bf16[32,16,3000]{2,1,0:T(8,128)(2,1)} %param.3) | copy-start | bytes 9216004
where the time goes:
time: 253 us; the launch traced here: 252 us
  other arithmetic  71.5 us (28%)
  blocking collectives  61.6 us (24%)
  local copies, waits for them, and re-layouts  61.5 us (24%)
  waiting for transfers between devices  26.3 us (10%)
  matrix products  22.5 us (9%)
  starting transfers between devices  8.26 us (3%)
    all_to_all x1, blocking collectives, body(): lax.all_to_all(white, 'chan', split_axis=2, concat_axis=3, tiled=True)  61.6 us
    convert_element_type x1, other arithmetic, dft_tables(): cosine = (taper[:, None] * jnp.cos(angle)).astype(jnp.bfloat16)  52.7 us
    all_to_all x1, waiting for transfers between devices, body(): lax.all_to_all(owned, 'tm', split_axis=2, concat_axis=0, tiled=True)  26.3 us
    unnamed x10, local copies, waits for them, and re-layouts  25.3 us
    all_to_all x2, local copies, waits for them, and re-layouts, body(): lax.all_to_all(white, 'chan', split_axis=2, concat_axis=3, tiled=True)  17 us
    another operation x2, local copies, waits for them, and re-layouts, body(): white = jnp.transpose(jnp.stack([white_re, white_im], axis=1), (0, 1, 3, 2))  10.2 us
    unnamed x1, other arithmetic  8.48 us
    dot_general x1, matrix products, body(): both = jnp.dot(sample_rows, table, preferred_element_type=jnp.float32)  8.39 us
  transfers between devices with their start and end apart: 1, of which 1 were waited for; matrix products, arithmetic and copies ran while one was open for 0% of the time, Pallas kernels for 0%

commit v1 on v0

v1 whole, which is shorter than its diff:
```python
import functools
import math

import jax
import jax.numpy as jnp
import numpy as np
from jax import lax
from jax.experimental import pallas as pl
from jax.experimental.pallas import tpu as pltpu
from jax.sharding import PartitionSpec as P

MESH = pl.DeviceIdType.MESH
F = 1024
LOW_BIN = 6
HALF_SPAN = 32
NT = 3000
NTP = 3072
DEVS = 256
PLANE = 32
BINS = 4
ROWS = 512
LANES = 256
CHUNKS = ROWS // LANES
Z_ORDER = (4, 0, 3, 5, 2, 6, 1, 7)
BF, F32 = jnp.bfloat16, jnp.float32


def tables():
    t = np.arange(NT, dtype=np.int64)
    k = LOW_BIN + np.arange(F, dtype=np.int64)
    angle = 2.0 * math.pi / NT * ((k[:, None] * t[None, :]) % NT)
    taper = 0.5 - 0.5 * np.cos(2.0 * math.pi / NT * t)
    re = (taper * np.cos(angle)).astype(np.float32)
    im = (-taper * np.sin(angle)).astype(np.float32)
    both = np.stack([re.reshape(DEVS, BINS, NT), im.reshape(DEVS, BINS, NT)], axis=1)
    out = np.zeros((2 * F, NTP), dtype=np.float32)
    out[:, :NT] = both.reshape(2 * F, NT)
    return out.astype(BF)


def me_at():
    ch, t = lax.axis_index("chan"), lax.axis_index("tm")
    return ch // 8, (ch // 2) % 4, (t // 2) * 2 + ch % 2, t % 2


def ids(z, x, y, c):
    return {"chan": z * 8 + x * 2 + y % 2, "tm": (y // 2) * 2 + c}


def linear(z, x, y, c):
    return (z * 8 + x * 2 + y % 2) * 4 + (y // 2) * 2 + c


def iota(shape, dim):
    return lax.broadcasted_iota(jnp.int32, shape, dim)


def front_kernel(x_hbm, t_hbm, valid_ref, d_hbm, xv, tv, xt, spec, amp, sendbuf, recv, perm, dbuf, x_sem, t_sem, send_sem, recv_sem, d_sem, sx, sy, sc):
    z, x, y, c = me_at()
    mine = linear(z, x, y, c)

    x_copies = [pltpu.make_async_copy(x_hbm.at[pl.ds(h * LANES, LANES)], xv.at[pl.ds(h * LANES, LANES)], x_sem.at[h]) for h in range(CHUNKS)]
    x_copies[0].start()

    def t_copy(b):
        rows = pl.ds(b * 256, 256)
        return pltpu.make_async_copy(t_hbm.at[rows], tv.at[rows], t_sem.at[b])

    for b in range(8):
        t_copy(b).start()
        if b == 0:
            x_copies[1].start()

    line_z = [((z + i) % 8, x, y, c) for i in range(1, 8)]
    line_x = [(z, (x + i) % 4, y, c) for i in range(1, 4)]
    line_y = [(z, x, (y + i) % 4, c) for i in range(1, 4)]
    line_c = [(z, x, y, 1 - c)]
    barrier = pltpu.get_barrier_semaphore()
    for q in line_z + line_x + line_y + line_c:
        pl.semaphore_signal(barrier, inc=1, device_id=ids(*q), device_id_type=MESH)

    def signal(line, sem):
        for q in line:
            pl.semaphore_signal(sem, inc=1, device_id=ids(*q), device_id_type=MESH)

    spread = (iota((16, LANES), 1) % 16 == iota((16, LANES), 0)).astype(F32)
    by_channel = jnp.dot(valid_ref[...].astype(F32), spread, preferred_element_type=F32)
    low = iota((1, 8, LANES), 1) < 4
    band = (jnp.abs(iota((128, 256), 0) + 64 - iota((128, 256), 1)) <= HALF_SPAN).astype(BF)
    amp[0:64, :] = jnp.zeros((64, LANES), BF)
    amp[64 + F:, :] = jnp.zeros((64, LANES), BF)
    xt[NTP - 128:, :] = jnp.zeros((128, ROWS), BF)

    def transform(h, first):
        lanes = slice(h * LANES, (h + 1) * LANES)
        x_copies[h].wait()
        for j in range(NT // 128):
            cols = slice(j * 128, (j + 1) * 128)
            xt[cols, lanes] = xv[lanes, cols].T
        tail = NT // 128 * 128
        xt[tail:NT, lanes] = xv[lanes, tail:NT].T

        def block(b, carry):
            if first:
                t_copy(b).wait()
            rows = pl.ds(pl.multiple_of(b * 256, 256), 256)
            out = jnp.dot(tv[rows, :], xt[:, lanes], preferred_element_type=F32)
            spec[rows, :] = out
            sq = (out * out).reshape(16, 2, 8, LANES)
            a, bb = sq[:, 0], sq[:, 1]
            total = jnp.where(low, a, bb) + pltpu.roll(jnp.where(low, bb, a), 4, 1)
            at = pl.ds(pl.multiple_of(64 + b * 128, 64), 128)
            amp[at, :] = jnp.sqrt(total).reshape(128, LANES).astype(BF)
            return carry

        lax.fori_loop(0, 8, block, 0)
        mask = iota((32, LANES), 0) == h * (LANES // 16) + iota((32, LANES), 1) // 16
        valid = jnp.sum(jnp.where(mask, by_channel, 0.0), axis=0, keepdims=True)

        def whiten(b, carry):
            total = jnp.dot(band, amp[pl.ds(pl.multiple_of(b * 128, 128), 256), :], preferred_element_type=F32)
            k = b * 128 + iota((128, LANES), 0)
            count = jnp.minimum(k + HALF_SPAN, F - 1) - jnp.maximum(k - HALF_SPAN, 0) + 1
            scale = (valid / (total / count.astype(F32) + 1e-6)).reshape(16, 8, LANES)
            turned = pltpu.roll(scale, 4, 1)
            s = spec[pl.ds(pl.multiple_of(b * 256, 256), 256), :].reshape(16, 2, 8, LANES)
            wa = s[:, 0] * jnp.where(low, scale, turned)
            wb = s[:, 1] * jnp.where(low, turned, scale)
            w = jnp.stack([wa, wb], axis=1)
            w = jnp.concatenate([w[..., :128], w[..., 128:]], axis=2)
            sendbuf[h, pl.ds(b * 32, 32)] = w.reshape(32, 16, 128).astype(BF)
            return carry

        lax.fori_loop(0, 8, whiten, 0)

    def send(h):
        own = pltpu.make_async_copy(sendbuf.at[h, mine], recv.at[h, mine], recv_sem.at[h, 0])
        own.start()
        for g in range(0, 8, 2):
            pair = Z_ORDER[g:g + 2]

            def one(n, carry):
                for off in pair:
                    q = ((z + off) % 8, (x + n // 8) % 4, (y + n // 2) % 4, (c + n) % 2)

                    def go():
                        pltpu.make_async_remote_copy(
                            src_ref=sendbuf.at[h, linear(*q)], dst_ref=recv.at[h, mine], send_sem=send_sem.at[h],
                            recv_sem=recv_sem.at[h, off], device_id=ids(*q), device_id_type=MESH).start()

                    if off == 0:
                        pl.when(n > 0)(go)
                    else:
                        go()
                return carry

            lax.fori_loop(0, PLANE, one, 0)

    transform(0, True)
    pl.semaphore_wait(barrier, 14)
    for line, sem in ((line_x, sx), (line_y, sy), (line_c, sc)):
        signal(line, sem)
        pl.semaphore_wait(sem, len(line))
    send(0)
    transform(1, False)
    send(1)

    frm, to = iota((1024, 1024), 0), iota((1024, 1024), 1)
    perm[...] = (to == (frm // 16 % 8) * 128 + (frm // 128) * 16 + frm % 16).astype(BF)
    r, p = iota((128, 128), 1), iota((128, 128), 0)
    row_perm = (p == (r % 4) * 32 + (r // 4 % 2) * 16 + r // 8).astype(BF)

    out_copies = []
    for g in range(8):
        off = Z_ORDER[g]
        zs = (z + 8 - off) % 8
        part = pl.ds(zs * PLANE, PLANE)
        for h in range(CHUNKS):
            pltpu.make_async_copy(sendbuf.at[h, pl.ds(0, PLANE)], recv.at[h, part], recv_sem.at[h, off]).wait()
        got = recv[:, part].reshape(CHUNKS, 8, 4, 16, 128)
        wide = jnp.concatenate([got[:, i].reshape(128, 128) for i in range(8)], axis=1)
        g1 = jnp.dot(row_perm, wide, preferred_element_type=F32).astype(BF)
        g2 = jnp.dot(g1, perm[...], preferred_element_type=F32).astype(BF)
        for f in range(BINS):
            for ri in range(2):
                for w in range(8):
                    dbuf[g, f, ri * 128 + w * 16:ri * 128 + w * 16 + 16, :] = g2[(f * 2 + ri) * 16:(f * 2 + ri) * 16 + 16, w * 128:w * 128 + 128]
        out = pltpu.make_async_copy(dbuf.at[g], d_hbm.at[:, zs], d_sem.at[g])
        out.start()
        out_copies.append(out)
    for out in out_copies:
        out.wait()
    for h in range(CHUNKS):
        pltpu.make_async_copy(sendbuf.at[h, pl.ds(0, DEVS - 1)], recv.at[h, pl.ds(0, DEVS - 1)], send_sem.at[h]).wait()


def cross_kernel(src_ref, d_ref, o_ref, pick, chosen):
    f, ri = pl.program_id(0), pl.program_id(1)

    @pl.when((f == 0) & (ri == 0))
    def _():
        pick[...] = (iota((1024, 512), 0) == src_ref[...]).astype(BF)

    def chans():
        return jnp.concatenate([d_ref[0, i] for i in range(8)], axis=1)

    @pl.when(ri == 0)
    def _():
        cc = chans()
        s = jnp.dot(cc, pick[...], preferred_element_type=F32).astype(BF)
        chosen[...] = s.T
        o_ref[0, 0] = jnp.dot(chosen[...], cc, preferred_element_type=F32).astype(BF)

    @pl.when(ri == 1)
    def _():
        cc = chans()
        cc = jnp.concatenate([cc[128:], -cc[:128]], axis=0)
        o_ref[0, 0] = jnp.dot(chosen[...], cc, preferred_element_type=F32).astype(BF)


def body(table, traces, valid, sources):
    rows = traces.reshape(ROWS, NT)
    any_spec = pl.BlockSpec(memory_space=pl.ANY)
    vmem = pl.BlockSpec(memory_space=pltpu.VMEM)
    d = pl.pallas_call(
        front_kernel,
        out_shape=jax.ShapeDtypeStruct((BINS, 8, 256, 128), BF),
        in_specs=[any_spec, any_spec, vmem],
        out_specs=any_spec,
        scratch_shapes=[
            pltpu.VMEM((ROWS, NT), BF),
            pltpu.VMEM((2 * F, NTP), BF),
            pltpu.VMEM((NTP, ROWS), BF),
            pltpu.VMEM((2 * F, LANES), F32),
            pltpu.VMEM((F + 128, LANES), BF),
            pltpu.VMEM((CHUNKS, DEVS, 16, 128), BF),
            pltpu.VMEM((CHUNKS, DEVS, 16, 128), BF),
            pltpu.VMEM((1024, 1024), BF),
            pltpu.VMEM((8, BINS, 256, 128), BF),
            pltpu.SemaphoreType.DMA((CHUNKS,)),
            pltpu.SemaphoreType.DMA((8,)),
            pltpu.SemaphoreType.DMA((CHUNKS,)),
            pltpu.SemaphoreType.DMA((CHUNKS, 8)),
            pltpu.SemaphoreType.DMA((8,)),
            pltpu.SemaphoreType.REGULAR,
            pltpu.SemaphoreType.REGULAR,
            pltpu.SemaphoreType.REGULAR,
        ],
        compiler_params=pltpu.CompilerParams(collective_id=0, has_side_effects=True, vmem_limit_bytes=56 * 2**20),
    )(rows, table, valid)
    return pl.pallas_call(
        cross_kernel,
        grid=(BINS, 2),
        out_shape=jax.ShapeDtypeStruct((2, BINS, 512, 1024), BF),
        in_specs=[pl.BlockSpec((1, 512), lambda f, r: (0, 0)), pl.BlockSpec((1, 8, 256, 128), lambda f, r: (f, 0, 0, 0))],
        out_specs=pl.BlockSpec((1, 1, 512, 1024), lambda f, r: (r, f, 0, 0)),
        scratch_shapes=[pltpu.VMEM((1024, 512), BF), pltpu.VMEM((512, 256), BF)],
        compiler_params=pltpu.CompilerParams(vmem_limit_bytes=48 * 2**20),
    )(sources.reshape(1, 512), d)


def solution(mesh):
    table = tables()

    def whole(traces, valid, sources):
        placed = (P(), P("tm", "chan", None), P("tm", "chan"), P())
        return jax.shard_map(
            body,
            mesh=mesh,
            in_specs=placed,
            out_specs=P(None, ("chan", "tm"), None, None),
            check_vma=False,
        )(jnp.asarray(table), traces, valid, sources)

    return whole
```

time: 253 us -> 85.8 us (0.34)
  Pallas kernels: 0 us -> 82.6 us
  other arithmetic: 71.5 us -> 0 us
  blocking collectives: 61.6 us -> 0 us
  local copies, waits for them, and re-layouts: 61.5 us -> 2.96 us
  waiting for transfers between devices: 26.3 us -> 0 us
  matrix products: 22.5 us -> 0 us
  starting transfers between devices: 8.26 us -> 0 us
    pallas_call x0 -> x2, Pallas kernels: none -> 82.6 us  [the longest x1 74.5 us: body(): pl.pallas_call(front_kernel, out_shape=jax.ShapeDtypeStruct((BINS, 8, 256...]
    all_to_all x1 -> x0, blocking collectives: 61.6 us -> none  [body(): lax.all_to_all(white, 'chan', split_axis=2, concat_axis=3, tiled=True)]
    convert_element_type x2 -> x0, other arithmetic: 53.5 us -> none  [the longest x1 52.7 us: dft_tables(): cosine = (taper[:, None] * jnp.cos(angle)).astype(jnp.bfloat16)]
    all_to_all x1 -> x0, waiting for transfers between devices: 26.3 us -> none  [body(): lax.all_to_all(owned, 'tm', split_axis=2, concat_axis=0, tiled=True)]
    dot_general x6 -> x0, matrix products: 22.5 us -> none  [the longest x1 8.39 us: body(): both = jnp.dot(sample_rows, table, preferred_element_type=jnp.float32)]
    unnamed x10 -> x5, local copies, waits for them, and re-layouts: 25.3 us -> 2.96 us
    all_to_all x4 -> x0, local copies, waits for them, and re-layouts: 21.4 us -> none  [the longest x2 17 us: body(): lax.all_to_all(white, 'chan', split_axis=2, concat_axis=3, tiled=True)]
    another operation x2 -> x0, local copies, waits for them, and re-layouts: 10.2 us -> none  [body(): white = jnp.transpose(jnp.stack([white_re, white_im], axis=1), (0, 1, 3, 2))]
  transfers between devices with their start and end apart: 1 -> 0, of which waited for: 1 -> 0; matrix products, arithmetic and copies ran while one was open for 0% -> 0% of each run, Pallas kernels for 0% -> 0%
where the time goes in v1:
time: 85.8 us; the launch traced here: 85.6 us
  Pallas kernels  82.6 us (96%)
  local copies, waits for them, and re-layouts  2.96 us (3%)
    pallas_call x1, Pallas kernels, body(): pl.pallas_call(front_kernel, out_shape=jax.ShapeDtypeStruct((BINS, 8, 256...  74.5 us
    pallas_call x1, Pallas kernels, body(): pl.pallas_call(cross_kernel, grid=(BINS, 2), out_shape=jax.ShapeDtypeStru...  8.09 us
    unnamed x5, local copies, waits for them, and re-layouts  2.96 us

profile of v1, /device:TPU:1, one launch (start us, length us, event | category | flops | bytes accessed | tf_op | source)
XLA Modules:
  0.0 85.6 jit_solution(17546615862472992523)
XLA Ops:
  0.0 1.4 %copy.5.valid_ref = s32[32,16]{1,0:T(8,128)} copy(s32[32,16]{0,1:T(8,128)} %param.5) | data formatting | bytes 4096 | tf_op args[1]
  1.4 0.0 copy-start.1
  1.4 74.5 %shard_map.46.d_ref = bf16[4,8,256,128]{3,2,1,0:T(8,128)(2,1)} custom-call(bf16[512,3000]{1,0:T(8,128)(2,1)} %bitcast.3, bf16[2048,3072]{1,0:T(8,128)(2,1)} %constant.2.clone.t_hbm, s32[32,16]{1,0:T(8,128)} %copy.5.valid_ref), custom_call_target="tpu_custom_call" | custom-call | tf_op jit(solution)/shard_map/pallas_call | solution.py:225
  75.9 0.0 copy-done.1
  75.9 0.0 copy-start
  75.9 1.6 %copy-done = bf16[4,8,256,128]{3,2,1,0:T(8,128)(2,1)S(1)} copy-done((bf16[4,8,256,128]{3,2,1,0:T(8,128)(2,1)S(1)}, bf16[4,8,256,128]{3,2,1,0:T(8,128)(2,1)}, u32[]{:S(2)}) %copy-start) | copy-done | bytes 2097176
  77.5 8.1 %shard_map.47 = bf16[2,4,512,1024]{3,2,1,0:T(8,128)(2,1)} custom-call(s32[1,512]{1,0:T(1,128)S(1)} %bitcast.2, bf16[4,8,256,128]{3,2,1,0:T(8,128)(2,1)S(1)} %copy-done), custom_call_target="tpu_custom_call" | custom-call | tf_op jit(solution)/shard_map/pallas_call | solution.py:251
Async XLA Ops:
  1.4 74.5 %copy-start.1 = (s32[512]{0:T(512)S(1)}, s32[512]{0:T(512)}, u32[]{:S(2)}) copy-start(s32[512]{0:T(512)} %param.6) | copy-start | bytes 6148
  75.9 1.6 %copy-start = (bf16[4,8,256,128]{3,2,1,0:T(8,128)(2,1)S(1)}, bf16[4,8,256,128]{3,2,1,0:T(8,128)(2,1)}, u32[]{:S(2)}) copy-start(bf16[4,8,256,128]{3,2,1,0:T(8,128)(2,1)} %shard_map.46.d_ref) | copy-start | bytes 6291460

commit v2 on v1

v2 whole, which is shorter than its diff:
```python
import functools
import math

import jax
import jax.numpy as jnp
import numpy as np
from jax import lax
from jax.experimental import pallas as pl
from jax.experimental.pallas import tpu as pltpu
from jax.sharding import PartitionSpec as P

MESH = pl.DeviceIdType.MESH
F = 1024
LOW_BIN = 6
HALF_SPAN = 32
NT = 3000
NTP = 3072
HALF = NTP // 2
DEVS = 256
PLANE = 32
BINS = 4
ROWS = 512
LANES = 256
CHUNKS = ROWS // LANES
PHASES = ((4, 1), (3, 7), (5, 0), (2, 6))
ARRIVAL = (4, 1, 7, 3, 5, 0, 2, 6)
BF, F32 = jnp.bfloat16, jnp.float32


def tables():
    t = np.arange(HALF, dtype=np.int64)
    k = LOW_BIN + np.arange(F, dtype=np.int64)
    angle = 2.0 * math.pi / NT * ((k[:, None] * t[None, :]) % NT)
    taper = 0.5 - 0.5 * np.cos(2.0 * math.pi / NT * t)
    weight = np.where(t < NT // 2, 1.0, np.where(t == NT // 2, 0.5, 0.0)) * taper
    return np.stack([weight * np.cos(angle), -weight * np.sin(angle)]).astype(np.float32).astype(BF)


def me_at():
    ch, t = lax.axis_index("chan"), lax.axis_index("tm")
    return ch // 8, (ch // 2) % 4, (t // 2) * 2 + ch % 2, t % 2


def ids(z, x, y, c):
    return {"chan": z * 8 + x * 2 + y % 2, "tm": (y // 2) * 2 + c}


def linear(z, x, y, c):
    return (z * 8 + x * 2 + y % 2) * 4 + (y // 2) * 2 + c


def iota(shape, dim):
    return lax.broadcasted_iota(jnp.int32, shape, dim)


def front_kernel(x_hbm, t_hbm, valid_ref, src_ref, d_hbm, s_hbm, xv, tv, xt, plus, minus, spec, amp, inv, sendbuf, recv, perm, pick, dbuf, chosen, x_sem, t_sem, send_sem, recv_sem, d_sem, s_sem, here):
    z, x, y, c = me_at()
    mine = linear(z, x, y, c)
    sign = 1 - 2 * c

    def plane_at(i):
        return lax.rem(z + 12 + sign * i, 8)

    x_copies = [pltpu.make_async_copy(x_hbm.at[pl.ds(h * LANES, LANES)], xv.at[pl.ds(h * LANES, LANES)], x_sem.at[h]) for h in range(CHUNKS)]
    x_copies[0].start()

    def t_copy(i):
        rows = pl.ds(pl.multiple_of(plane_at(i - 1) * 128, 128), 128)
        return pltpu.make_async_copy(t_hbm.at[:, rows], tv.at[:, rows], t_sem.at[i])

    for i in range(8):
        t_copy(i).start()
    x_copies[1].start()

    column = [((z + i) % 8, x, y, (c + j) % 2) for i in range(8) for j in range(2) if i or j]
    plane = [(z, (x + i) % 4, (y + j) % 4, c) for i in range(4) for j in range(4) if i or j]
    barrier = pltpu.get_barrier_semaphore()
    for q in column + plane:
        pl.semaphore_signal(barrier, inc=1, device_id=ids(*q), device_id_type=MESH)

    spread = (iota((16, LANES), 1) % 16 == iota((16, LANES), 0)).astype(F32)
    by_channel = lax.dot_general(valid_ref[...].astype(F32), spread, (((0,), (0,)), ((), ())), preferred_element_type=F32)
    low = iota((1, 8, LANES), 1) < 4
    band = (jnp.abs(iota((128, 256), 0) + 64 - iota((128, 256), 1)) <= HALF_SPAN).astype(BF)
    back = (iota((128, 256), 0) + iota((128, 256), 1) == NT - 22 * 128).astype(BF)
    k = iota((F, LANES), 0)
    inv[...] = 1.0 / (jnp.minimum(k + HALF_SPAN, F - 1) - jnp.maximum(k - HALF_SPAN, 0) + 1).astype(F32)
    amp[0:64, :] = jnp.zeros((64, LANES), BF)
    amp[64 + F:, :] = jnp.zeros((64, LANES), BF)
    xt[NTP - 128:, :] = jnp.zeros((128, ROWS), BF)

    def fold(h):
        lanes = slice(h * LANES, (h + 1) * LANES)
        x_copies[h].wait()
        for j in range(NT // 128):
            cols = slice(j * 128, (j + 1) * 128)
            xt[cols, lanes] = xv[lanes, cols].T
        tail = NT // 128 * 128
        xt[tail:NT, lanes] = xv[lanes, tail:NT].T
        for m in range(HALF // 128):
            at, there = slice(m * 128, m * 128 + 128), (22 - m) * 128
            ahead = xt[at, lanes].astype(F32)
            behind = jnp.dot(back, xt[there:there + 256, lanes], preferred_element_type=F32)
            for total, out in ((ahead + behind, plus), (ahead - behind, minus)):
                rounded = total.astype(BF)
                out[at, :LANES] = rounded
                out[at, LANES:] = (total - rounded.astype(F32)).astype(BF)

    def block(first, n):
        rows = pl.ds(first, n)
        re = jnp.dot(tv[0, rows, :], plus[...], preferred_element_type=F32)
        im = jnp.dot(tv[1, rows, :], minus[...], preferred_element_type=F32)
        re = re[:, :LANES] + re[:, LANES:]
        im = im[:, :LANES] + im[:, LANES:]
        spec[0, rows, :] = re
        spec[1, rows, :] = im
        power = re * re + im * im
        amp[pl.ds(pl.multiple_of(64 + first, 64), n), :] = (power * lax.rsqrt(jnp.maximum(power, 1e-37))).astype(BF)

    def valid_row(h):
        mask = iota((32, LANES), 0) == h * (LANES // 16) + iota((32, LANES), 1) // 16
        return jnp.sum(jnp.where(mask, by_channel, 0.0), axis=0, keepdims=True)

    def whiten(h, b, valid):
        rows = pl.ds(pl.multiple_of(b * 128, 128), 128)
        total = jnp.dot(band, amp[pl.ds(pl.multiple_of(b * 128, 128), 256), :], preferred_element_type=F32)
        scale = valid / (total * inv[rows, :] + 1e-6)
        wr = (spec[0, rows, :] * scale).reshape(16, 8, LANES)
        wi = (spec[1, rows, :] * scale).reshape(16, 8, LANES)
        wa = jnp.where(low, wr, pltpu.roll(wi, 4, 1))
        wb = jnp.where(low, pltpu.roll(wr, 4, 1), wi)
        w = jnp.stack([wa, wb], axis=1)
        w = jnp.concatenate([w[..., :128], w[..., 128:]], axis=2)
        sendbuf[h, pl.ds(b * 32, 32)] = w.reshape(32, 16, 128).astype(BF)

    xs = [lax.rem(x + i, 4) for i in range(4)]
    ys = [lax.rem(y + i, 4) for i in range(4)]
    cs = [c, 1 - c]
    spots = [(xs[i] * 2 + lax.rem(ys[j], 2), lax.div(ys[j], 2) * 2 + cs[n]) for i in range(4) for j in range(4) for n in range(2)]

    def send(h, n, to, group):
        chan, tm = spots[n]
        chan = to * 8 + chan
        pltpu.make_async_remote_copy(
            src_ref=sendbuf.at[h, chan * 4 + tm], dst_ref=recv.at[h, mine], send_sem=send_sem.at[h],
            recv_sem=recv_sem.at[h, group], device_id={"chan": chan, "tm": tm}, device_id_type=MESH).start()

    fold(0)
    pl.semaphore_wait(barrier, 30)
    for q in plane:
        pl.semaphore_signal(here, inc=1, device_id=ids(*q), device_id_type=MESH)
    valid = valid_row(0)

    def step(i, carry):
        @pl.when(i < 8)
        def _():
            t_copy(i).wait()
            block(pl.multiple_of(plane_at(i - 1) * 128, 128), 128)

        @pl.when(i >= 2)
        def _():
            to = plane_at(i - 2)
            whiten(0, to, valid)

            @pl.when(i == 2)
            def _():
                pl.semaphore_wait(here, 15)

            group = lax.rem(to + 8 - z, 8)

            @pl.when(group > 0)
            def _():
                send(0, 0, to, group)

            for n in range(1, PLANE):
                send(0, n, to, group)

        return carry

    lax.fori_loop(0, 10, step, 0)
    pltpu.make_async_copy(sendbuf.at[0, mine], recv.at[0, mine], recv_sem.at[0, 0]).start()

    fold(1)

    def wide_block(b, carry):
        block(pl.multiple_of(b * 256, 256), 256)
        return carry

    lax.fori_loop(0, 4, wide_block, 0)
    valid = valid_row(1)

    def whiten_1(b, carry):
        whiten(1, b, valid)
        return carry

    lax.fori_loop(0, 8, whiten_1, 0)
    pltpu.make_async_copy(sendbuf.at[1, mine], recv.at[1, mine], recv_sem.at[1, 0]).start()
    for pair in PHASES:
        groups = [lax.rem(8 + sign * off, 8) for off in pair]
        planes = [lax.rem(z + g, 8) for g in groups]
        for n in range(PLANE):
            for off, g, to in zip(pair, groups, planes):
                if off or n:
                    send(1, n, to, g)

    frm, to = iota((1024, 1024), 0), iota((1024, 1024), 1)
    perm[...] = (to == (frm // 16 % 8) * 128 + (frm // 128) * 16 + frm % 16).astype(BF)
    r, p = iota((128, 128), 1), iota((128, 128), 0)
    row_perm = (p == (r % 4) * 32 + (r // 4 % 2) * 16 + r // 8).astype(BF)
    for i in range(8):
        pick[i] = (iota((128, 512), 0) + i * 128 == src_ref[...]).astype(BF).T

    out_copies = []
    for g in range(8):
        off = ARRIVAL[g]
        zs = lax.rem(z + 8 - off, 8)
        part = pl.ds(zs * PLANE, PLANE)
        for h in range(CHUNKS):
            pltpu.make_async_copy(sendbuf.at[h, pl.ds(0, PLANE)], recv.at[h, part], recv_sem.at[h, off]).wait()
        got = recv[:, part].reshape(CHUNKS, 8, 4, 16, 128)
        wide = jnp.concatenate([got[:, i].reshape(128, 128) for i in range(8)], axis=1)
        g1 = jnp.dot(row_perm, wide, preferred_element_type=F32).astype(BF)
        g2 = jnp.dot(g1, perm[...], preferred_element_type=F32).astype(BF)
        for f in range(BINS):
            bin_rows = []
            for ri in range(2):
                rows = slice((f * 2 + ri) * 16, (f * 2 + ri) * 16 + 16)
                bin_rows += [g2[rows, w * 128:w * 128 + 128] for w in range(8)]
            mat = jnp.concatenate(bin_rows, axis=0)
            dbuf[g, f] = mat
            chan_part = lax.dot_general(pick[zs], mat, (((1,), (1,)), ((), ())), preferred_element_type=F32).astype(BF)
            chosen[f] = chan_part if g == 0 else chosen[f] + chan_part
        out = pltpu.make_async_copy(dbuf.at[g], d_hbm.at[:, zs], d_sem.at[g])
        out.start()
        out_copies.append(out)
    out = pltpu.make_async_copy(chosen, s_hbm, s_sem)
    out.start()
    for out in out_copies + [out]:
        out.wait()
    for h in range(CHUNKS):
        pltpu.make_async_copy(sendbuf.at[h, pl.ds(0, DEVS - 1)], recv.at[h, pl.ds(0, DEVS - 1)], send_sem.at[h]).wait()


def cross_kernel(d_hbm, s_hbm, o_hbm, dv, chosen, buf, d_sem, s_sem, o_sem):
    copies = []
    for f in range(BINS):
        copies.append((pltpu.make_async_copy(d_hbm.at[f], dv.at[f], d_sem.at[f]), pltpu.make_async_copy(s_hbm.at[f], chosen.at[f], s_sem.at[f])))
        for copy in copies[-1]:
            copy.start()
    outs = []
    for f in range(BINS):
        for copy in copies[f]:
            copy.wait()
        cc = jnp.concatenate([dv[f, i] for i in range(8)], axis=1)
        for ri in range(2):
            if ri == 1:
                cc = jnp.concatenate([cc[128:], -cc[:128]], axis=0)
            for m in range(0, 512, 256):
                part = pl.ds(m, 256)
                buf[ri, f, part] = jnp.dot(chosen[f, part, :], cc, preferred_element_type=F32).astype(BF)
                out = pltpu.make_async_copy(buf.at[ri, f, part], o_hbm.at[ri, f, part], o_sem.at[ri, f, m // 256])
                out.start()
                outs.append(out)
    for out in outs:
        out.wait()


def body(table, traces, valid, sources):
    rows = traces.reshape(ROWS, NT)
    any_spec = pl.BlockSpec(memory_space=pl.ANY)
    vmem = pl.BlockSpec(memory_space=pltpu.VMEM)
    d, s = pl.pallas_call(
        front_kernel,
        out_shape=(jax.ShapeDtypeStruct((BINS, 8, 256, 128), BF), jax.ShapeDtypeStruct((BINS, 512, 256), BF)),
        in_specs=[any_spec, any_spec, vmem, vmem],
        out_specs=(any_spec, any_spec),
        scratch_shapes=[
            pltpu.VMEM((ROWS, NT), BF),
            pltpu.VMEM((2, F, HALF), BF),
            pltpu.VMEM((NTP, ROWS), BF),
            pltpu.VMEM((HALF, 2 * LANES), BF),
            pltpu.VMEM((HALF, 2 * LANES), BF),
            pltpu.VMEM((2, F, LANES), F32),
            pltpu.VMEM((F + 128, LANES), BF),
            pltpu.VMEM((F, LANES), F32),
            pltpu.VMEM((CHUNKS, DEVS, 16, 128), BF),
            pltpu.VMEM((CHUNKS, DEVS, 16, 128), BF),
            pltpu.VMEM((1024, 1024), BF),
            pltpu.VMEM((8, 512, 128), BF),
            pltpu.VMEM((8, BINS, 256, 128), BF),
            pltpu.VMEM((BINS, 512, 256), BF),
            pltpu.SemaphoreType.DMA((CHUNKS,)),
            pltpu.SemaphoreType.DMA((8,)),
            pltpu.SemaphoreType.DMA((CHUNKS,)),
            pltpu.SemaphoreType.DMA((CHUNKS, 8)),
            pltpu.SemaphoreType.DMA((8,)),
            pltpu.SemaphoreType.DMA,
            pltpu.SemaphoreType.REGULAR,
        ],
        compiler_params=pltpu.CompilerParams(collective_id=0, has_side_effects=True, vmem_limit_bytes=58 * 2**20),
    )(rows, table, valid.T, sources.reshape(1, 512))
    return pl.pallas_call(
        cross_kernel,
        out_shape=jax.ShapeDtypeStruct((2, BINS, 512, 1024), BF),
        in_specs=[any_spec, any_spec],
        out_specs=any_spec,
        scratch_shapes=[
            pltpu.VMEM((BINS, 8, 256, 128), BF),
            pltpu.VMEM((BINS, 512, 256), BF),
            pltpu.VMEM((2, BINS, 512, 1024), BF),
            pltpu.SemaphoreType.DMA((BINS,)),
            pltpu.SemaphoreType.DMA((BINS,)),
            pltpu.SemaphoreType.DMA((2, BINS, 2)),
        ],
        compiler_params=pltpu.CompilerParams(vmem_limit_bytes=60 * 2**20),
    )(d, s)


def solution(mesh):
    table = tables()

    def whole(traces, valid, sources):
        placed = (P(), P("tm", "chan", None), P("tm", "chan"), P())
        return jax.shard_map(
            body,
            mesh=mesh,
            in_specs=placed,
            out_specs=P(None, ("chan", "tm"), None, None),
            check_vma=False,
        )(jnp.asarray(table), traces, valid, sources)

    return whole
```

time: 85.8 us -> 71.3 us (0.83)
  Pallas kernels: 82.6 us -> 70.4 us
  local copies, waits for them, and re-layouts: 2.96 us -> 0 us
    pallas_call x2, Pallas kernels: 82.6 us -> 70.4 us  [the longest x1 65.4 us: body(): pl.pallas_call(front_kernel, out_shape=(jax.ShapeDtypeStruct((BINS, 8, 25...]
    unnamed x5 -> x0, local copies, waits for them, and re-layouts: 2.96 us -> none
where the time goes in v2:
time: 71.3 us; the launch traced here: 70.6 us
  Pallas kernels  70.4 us (99%)
    pallas_call x1, Pallas kernels, body(): pl.pallas_call(front_kernel, out_shape=(jax.ShapeDtypeStruct((BINS, 8, 25...  65.4 us
    pallas_call x1, Pallas kernels, body(): pl.pallas_call(cross_kernel, out_shape=jax.ShapeDtypeStruct((2, BINS, 512...  5.04 us

profile of v2, /device:TPU:1, one launch (start us, length us, event | category | flops | bytes accessed | tf_op | source)
XLA Modules:
  0.0 70.6 jit_solution(14645062046203702527)
XLA Ops:
  0.0 65.4 %shard_map.46 = (bf16[4,8,256,128]{3,2,1,0:T(8,128)(2,1)}, bf16[4,512,256]{2,1,0:T(8,128)(2,1)}) custom-call(bf16[512,3000]{1,0:T(8,128)(2,1)} %bitcast.3, bf16[2,1024,1536]{2,1,0:T(8,128)(2,1)} %constant.2.clone.t_hbm, s32[16,32]{1,0:T(8,128)} %bitcast.4, s32[1,512]{1,0:T(1,128)} %bitcast.5), custom_call_target="tpu_custom_call" | custom-call | tf_op jit(solution)/shard_map/pallas_call | solution.py:272
  65.4 5.0 %shard_map.47 = bf16[2,4,512,1024]{3,2,1,0:T(8,128)(2,1)} custom-call(bf16[4,8,256,128]{3,2,1,0:T(8,128)(2,1)} %get-tuple-element.7.d_hbm, bf16[4,512,256]{2,1,0:T(8,128)(2,1)} %get-tuple-element.8.s_hbm), custom_call_target="tpu_custom_call" | custom-call | tf_op jit(solution)/shard_map/pallas_call | solution.py:302

commit v3 on v2

v3 whole, which is shorter than its diff:
```python
import functools
import math

import jax
import jax.numpy as jnp
import numpy as np
from jax import lax
from jax.experimental import pallas as pl
from jax.experimental.pallas import tpu as pltpu
from jax.sharding import PartitionSpec as P

MESH = pl.DeviceIdType.MESH
F = 1024
LOW_BIN = 6
HALF_SPAN = 32
NT = 3000
NTP = 3072
HALF = NTP // 2
EDGE = 64
FAR = 4
DEVS = 256
PLANE = 32
BINS = 4
ROWS = 512
LANES = 256
CHUNKS = ROWS // LANES
PHASES = ((4, 1), (3, 7), (5, 0), (2, 6))
ARRIVAL = ((4,), (1, 7), (3, 5), (0,), (2, 6))
BF, F32 = jnp.bfloat16, jnp.float32


def tables():
    t = np.arange(HALF, dtype=np.int64)
    k = LOW_BIN + np.arange(F, dtype=np.int64)
    angle = 2.0 * math.pi / NT * ((k[:, None] * t[None, :]) % NT)
    taper = 0.5 - 0.5 * np.cos(2.0 * math.pi / NT * t)
    weight = np.where(t < NT // 2, 1.0, np.where(t == NT // 2, 0.5, 0.0)) * taper
    both = np.stack([weight * np.cos(angle), -weight * np.sin(angle)]).astype(np.float32)
    return np.pad(both, ((0, 0), (EDGE, EDGE), (0, 0))).astype(BF)


def me_at():
    ch, t = lax.axis_index("chan"), lax.axis_index("tm")
    return ch // 8, (ch // 2) % 4, (t // 2) * 2 + ch % 2, t % 2


def ids(z, x, y, c):
    return {"chan": z * 8 + x * 2 + y % 2, "tm": (y // 2) * 2 + c}


def linear(z, x, y, c):
    return (z * 8 + x * 2 + y % 2) * 4 + (y // 2) * 2 + c


def iota(shape, dim):
    return lax.broadcasted_iota(jnp.int32, shape, dim)


def front_kernel(x_hbm, t_hbm, small_ref, d_ref, s_ref, xv, tv, tv_first, xt, plus, minus, spec, amp, inv, sendbuf, recv, pick, x_sem, t_sem, send_sem, recv_sem, here):
    z, x, y, c = me_at()
    mine = linear(z, x, y, c)
    sign = 1 - 2 * c
    far = lax.rem(z + FAR, 8)

    x_copies = [pltpu.make_async_copy(x_hbm.at[pl.ds(h * LANES, LANES)], xv.at[pl.ds(h * LANES, LANES)], x_sem.at[h]) for h in range(CHUNKS)]
    first_rows = pl.ds(pl.multiple_of(far * 128 + EDGE - HALF_SPAN, 32), 128 + 2 * HALF_SPAN)
    first_copy = pltpu.make_async_copy(t_hbm.at[:, first_rows], tv_first, t_sem.at[4])

    def t_copy(b):
        rows = pl.ds(EDGE + b * 256, 256)
        return pltpu.make_async_copy(t_hbm.at[:, rows], tv.at[:, rows], t_sem.at[b])

    x_copies[0].start()
    first_copy.start()

    column = [((z + i) % 8, x, y, (c + j) % 2) for i in range(8) for j in range(2) if i or j]
    plane = [(z, (x + i) % 4, (y + j) % 4, c) for i in range(4) for j in range(4) if i or j]
    barrier = pltpu.get_barrier_semaphore()
    for q in column + plane:
        pl.semaphore_signal(barrier, inc=1, device_id=ids(*q), device_id_type=MESH)

    spread = (iota((16, LANES), 1) % 16 == iota((16, LANES), 0)).astype(F32)
    by_channel = lax.dot_general(small_ref[0:16, 0:32].astype(F32), spread, (((0,), (0,)), ((), ())), preferred_element_type=F32)
    low = iota((1, 8, LANES), 1) < 4
    band = (jnp.abs(iota((128, 256), 0) + 64 - iota((128, 256), 1)) <= HALF_SPAN).astype(BF)
    back = (iota((128, 256), 0) + iota((128, 256), 1) == NT - 22 * 128).astype(BF)
    k = iota((F, LANES), 0)
    inv[...] = 1.0 / (jnp.minimum(k + HALF_SPAN, F - 1) - jnp.maximum(k - HALF_SPAN, 0) + 1).astype(F32)
    amp[:EDGE, :] = jnp.zeros((EDGE, LANES), BF)
    amp[EDGE + F:, :] = jnp.zeros((EDGE, LANES), BF)
    xt[NTP - 128:, :] = jnp.zeros((128, ROWS), BF)

    def fold(h):
        lanes = slice(h * LANES, (h + 1) * LANES)
        x_copies[h].wait()
        for j in range(NT // 128):
            cols = slice(j * 128, (j + 1) * 128)
            xt[cols, lanes] = xv[lanes, cols].T
        tail = NT // 128 * 128
        xt[tail:NT, lanes] = xv[lanes, tail:NT].T
        for m in range(HALF // 128):
            at, there = slice(m * 128, m * 128 + 128), (22 - m) * 128
            ahead = xt[at, lanes].astype(F32)
            behind = jnp.dot(back, xt[there:there + 256, lanes], preferred_element_type=F32)
            for total, out in ((ahead + behind, plus), (ahead - behind, minus)):
                rounded = total.astype(BF)
                out[at, :LANES] = rounded
                out[at, LANES:] = (total - rounded.astype(F32)).astype(BF)

    def block(table, first, n):
        rows = pl.ds(first, n)
        re = jnp.dot(table[0], plus[...], preferred_element_type=F32)
        im = jnp.dot(table[1], minus[...], preferred_element_type=F32)
        re = re[:, :LANES] + re[:, LANES:]
        im = im[:, :LANES] + im[:, LANES:]
        spec[0, rows, :] = re
        spec[1, rows, :] = im
        power = re * re + im * im
        amp[rows, :] = (power * lax.rsqrt(jnp.maximum(power, 1e-37))).astype(BF)

    def valid_row(h):
        mask = iota((32, LANES), 0) == h * (LANES // 16) + iota((32, LANES), 1) // 16
        return jnp.sum(jnp.where(mask, by_channel, 0.0), axis=0, keepdims=True)

    def whiten(h, b, valid):
        at = pl.multiple_of(b * 128, 128)
        rows = pl.ds(pl.multiple_of(EDGE + at, EDGE), 128)
        total = jnp.dot(band, amp[pl.ds(at, 256), :], preferred_element_type=F32)
        scale = valid / (total * inv[pl.ds(at, 128), :] + 1e-6)
        wr = (spec[0, rows, :] * scale).reshape(16, 8, LANES)
        wi = (spec[1, rows, :] * scale).reshape(16, 8, LANES)
        wa = jnp.where(low, wr, pltpu.roll(wi, 4, 1))
        wb = jnp.where(low, pltpu.roll(wr, 4, 1), wi)
        w = jnp.stack([wa, wb], axis=1)
        w = jnp.concatenate([w[..., :128], w[..., 128:]], axis=2)
        sendbuf[h, pl.ds(b * 32, 32)] = w.reshape(32, 16, 128).astype(BF)

    def send(h, n, off):
        xn, yn = lax.rem(x + lax.div(n, 8), 4), lax.rem(y + lax.rem(lax.div(n, 2), 4), 4)
        chan = lax.rem(z + off, 8) * 8 + xn * 2 + lax.rem(yn, 2)
        tm = lax.div(yn, 2) * 2 + lax.rem(c + n, 2)
        pltpu.make_async_remote_copy(
            src_ref=sendbuf.at[h, chan * 4 + tm], dst_ref=recv.at[h, mine], send_sem=send_sem.at[h],
            recv_sem=recv_sem.at[h, off], device_id={"chan": chan, "tm": tm}, device_id_type=MESH).start()

    def send_planes(h, offs):
        def one(n, carry):
            for off in offs:
                if isinstance(off, int) and off == 0:
                    pl.when(n > 0)(functools.partial(send, h, n, 0))
                else:
                    send(h, n, off)
            return carry

        lax.fori_loop(0, PLANE, one, 0)
        if any(isinstance(off, int) and off == 0 for off in offs):
            pltpu.make_async_copy(sendbuf.at[h, mine], recv.at[h, mine], recv_sem.at[h, 0]).start()

    def relay():
        pl.semaphore_wait(barrier, 30)
        for q in plane:
            pl.semaphore_signal(here, inc=1, device_id=ids(*q), device_id_type=MESH)

    pl.when(z >= 4)(relay)
    fold(0)
    for b in range(4):
        t_copy(b).start()
    x_copies[1].start()
    valid = valid_row(0)
    first_copy.wait()
    block(tv_first, pl.multiple_of(far * 128 + EDGE - HALF_SPAN, 32), 128 + 2 * HALF_SPAN)
    whiten(0, far, valid)
    pl.when(z < 4)(relay)
    pl.semaphore_wait(here, 15)
    send_planes(0, (FAR,))

    def rest(h, valid):
        def wide_block(b, carry):
            if h == 0:
                t_copy(b).wait()
            at = pl.multiple_of(EDGE + b * 256, EDGE)
            block(tv.at[:, pl.ds(at, 256)], at, 256)
            return carry

        lax.fori_loop(0, 4, wide_block, 0)

        def whiten_one(b, carry):
            if h == 0:
                pl.when(b != far)(lambda: whiten(h, b, valid))
            else:
                whiten(h, b, valid)
            return carry

        lax.fori_loop(0, 8, whiten_one, 0)

    rest(0, valid)
    send_planes(0, (3, 5, 1, 7, 2, 6, 0))
    fold(1)
    rest(1, valid_row(1))
    for pair in PHASES:
        send_planes(1, [off if off == 0 else lax.rem(8 + sign * off, 8) for off in pair])

    r, p = iota((128, 128), 1), iota((128, 128), 0)
    row_perm = (p == (r % 4) * 32 + (r // 4 % 2) * 16 + r // 8).astype(BF)
    for i in range(8):
        pick[i] = (iota((128, 512), 0) + i * 128 == small_ref[16:17, :]).astype(BF).T

    group = iota((128, 128), 1) // 16

    def swap(tiles):
        for bit in (4, 2, 1):
            high = group // bit % 2 == 1
            for i in range(8):
                if not i & bit:
                    a, b = tiles[i], tiles[i | bit]
                    tiles[i] = jnp.where(high, pltpu.roll(b, 16 * bit, 1), a)
                    tiles[i | bit] = jnp.where(high, b, pltpu.roll(a, 128 - 16 * bit, 1))
        return tiles

    for offs in ARRIVAL:
        places = [lax.rem(z + 8 - off, 8) for off in offs]
        mats = []
        for off, zs in zip(offs, places):
            part = pl.ds(zs * PLANE, PLANE)
            for h in range(CHUNKS):
                pltpu.make_async_copy(sendbuf.at[h, pl.ds(0, PLANE)], recv.at[h, part], recv_sem.at[h, off]).wait()
            got = recv[:, part].reshape(CHUNKS, 8, 4, 16, 128)
            wide = jnp.concatenate([got[:, i].reshape(128, 128) for i in range(8)], axis=1)
            ordered = jnp.dot(row_perm, wide, preferred_element_type=F32)
            tiles = [t.astype(BF) for t in swap([ordered[:, i * 128:i * 128 + 128] for i in range(8)])]
            bins = []
            for f in range(BINS):
                at = [(f * 2 + ri) * 16 for ri in range(2)]
                bins.append(jnp.concatenate([t[r:r + 16] for r in at for t in tiles], axis=0))
                d_ref[f, zs] = bins[f]
            mats.append(bins)
        picks = jnp.concatenate([pick[zs] for zs in places], axis=1)
        for f in range(BINS):
            mat = jnp.concatenate([bins[f] for bins in mats], axis=1)
            chosen = lax.dot_general(picks, mat, (((1,), (1,)), ((), ())), preferred_element_type=F32).astype(BF)
            s_ref[f] = chosen if offs == ARRIVAL[0] else s_ref[f] + chosen
    for h in range(CHUNKS):
        pltpu.make_async_copy(sendbuf.at[h, pl.ds(0, DEVS - 1)], recv.at[h, pl.ds(0, DEVS - 1)], send_sem.at[h]).wait()


def cross_kernel(d_ref, s_ref, o_hbm, buf, o_sem):
    outs = []
    for f in range(BINS):
        cc = jnp.concatenate([d_ref[f, i] for i in range(8)], axis=1)
        for ri in range(2):
            if ri == 1:
                cc = jnp.concatenate([cc[128:], -cc[:128]], axis=0)
            for m in range(0, 512, 256):
                part = pl.ds(m, 256)
                buf[ri, f, part] = jnp.dot(s_ref[f, part, :], cc, preferred_element_type=F32).astype(BF)
                out = pltpu.make_async_copy(buf.at[ri, f, part], o_hbm.at[ri, f, part], o_sem.at[ri, f, m // 256])
                out.start()
                outs.append(out)
    for out in outs:
        out.wait()


def body(table, traces, valid, sources):
    rows = traces.reshape(ROWS, NT)
    small = jnp.pad(valid.T, ((0, 8), (0, 480))) + jnp.pad(sources.reshape(1, 512), ((16, 7), (0, 0)))
    any_spec = pl.BlockSpec(memory_space=pl.ANY)
    vmem = pl.BlockSpec(memory_space=pltpu.VMEM)
    hbm = pl.BlockSpec(memory_space=pltpu.HBM)
    d, s = pl.pallas_call(
        front_kernel,
        out_shape=(jax.ShapeDtypeStruct((BINS, 8, 256, 128), BF), jax.ShapeDtypeStruct((BINS, 512, 256), BF)),
        in_specs=[hbm, hbm, vmem],
        out_specs=(vmem, vmem),
        scratch_shapes=[
            pltpu.VMEM((ROWS, NT), BF),
            pltpu.VMEM((2, F + 2 * EDGE, HALF), BF),
            pltpu.VMEM((2, 128 + 2 * HALF_SPAN, HALF), BF),
            pltpu.VMEM((NTP, ROWS), BF),
            pltpu.VMEM((HALF, 2 * LANES), BF),
            pltpu.VMEM((HALF, 2 * LANES), BF),
            pltpu.VMEM((2, F + 2 * EDGE, LANES), F32),
            pltpu.VMEM((F + 2 * EDGE, LANES), BF),
            pltpu.VMEM((F, LANES), F32),
            pltpu.VMEM((CHUNKS, DEVS, 16, 128), BF),
            pltpu.VMEM((CHUNKS, DEVS, 16, 128), BF),
            pltpu.VMEM((8, 512, 128), BF),
            pltpu.SemaphoreType.DMA((CHUNKS,)),
            pltpu.SemaphoreType.DMA((5,)),
            pltpu.SemaphoreType.DMA((CHUNKS,)),
            pltpu.SemaphoreType.DMA((CHUNKS, 8)),
            pltpu.SemaphoreType.REGULAR,
        ],
        compiler_params=pltpu.CompilerParams(collective_id=0, has_side_effects=True, vmem_limit_bytes=48 * 2**20),
    )(rows, table, small)
    return pl.pallas_call(
        cross_kernel,
        out_shape=jax.ShapeDtypeStruct((2, BINS, 512, 1024), BF),
        in_specs=[vmem, vmem],
        out_specs=any_spec,
        scratch_shapes=[
            pltpu.VMEM((2, BINS, 512, 1024), BF),
            pltpu.SemaphoreType.DMA((2, BINS, 2)),
        ],
        compiler_params=pltpu.CompilerParams(vmem_limit_bytes=24 * 2**20),
    )(d, s)


def solution(mesh):
    table = tables()

    def whole(traces, valid, sources):
        placed = (P(), P("tm", "chan", None), P("tm", "chan"), P())
        return jax.shard_map(
            body,
            mesh=mesh,
            in_specs=placed,
            out_specs=P(None, ("chan", "tm"), None, None),
            check_vma=False,
        )(jnp.asarray(table), traces, valid, sources)

    return whole
```

time: 71.3 us -> 69 us (0.968)
  Pallas kernels: 70.4 us -> 68 us
  other arithmetic: 0 us -> 0.72 us
    pallas_call x1, Pallas kernels: 5.04 us -> 3.72 us  [body(): pl.pallas_call(cross_kernel, out_shape=jax.ShapeDtypeStruct((2, BINS, 512...]
    pallas_call x1, Pallas kernels: 65.4 us -> 64.2 us  [body(): pl.pallas_call(front_kernel, out_shape=(jax.ShapeDtypeStruct((BINS, 8, 25...]
    add x0 -> x1, other arithmetic: none -> 0.72 us  [body(): jnp.pad(valid.T, ((0, 8), (0, 480)))]
where the time goes in v3:
time: 69 us; the launch traced here: 68.9 us
  Pallas kernels  68 us (99%)
  other arithmetic  0.72 us (1%)
    pallas_call x1, Pallas kernels, body(): pl.pallas_call(front_kernel, out_shape=(jax.ShapeDtypeStruct((BINS, 8, 25...  64.2 us
    pallas_call x1, Pallas kernels, body(): pl.pallas_call(cross_kernel, out_shape=jax.ShapeDtypeStruct((2, BINS, 512...  3.72 us

profile of v3, /device:TPU:1, one launch (start us, length us, event | category | flops | bytes accessed | tf_op | source)
XLA Modules:
  0.0 68.9 jit_solution(4469679165268883370)
XLA Ops:
  0.0 0.7 %pad_add_fusion.small_ref = s32[24,512]{1,0:T(8,128)S(1)} fusion(s32[1,512]{1,0:T(1,128)} %bitcast.5, s32[16,32]{1,0:T(8,128)} %bitcast.4), kind=kLoop, calls=%fused_computation | loop fusion | flops 12288 | bytes 53248 | tf_op jit(solution)/shard_map/add | solution.py:265
  0.7 64.2 %shard_map.46 = (bf16[4,8,256,128]{3,2,1,0:T(8,128)(2,1)S(1)}, bf16[4,512,256]{2,1,0:T(8,128)(2,1)S(1)}) custom-call(bf16[512,3000]{1,0:T(8,128)(2,1)} %bitcast.3, bf16[2,1152,1536]{2,1,0:T(8,128)(2,1)} %constant.4.clone.t_hbm, s32[24,512]{1,0:T(8,128)S(1)} %pad_add_fusion.small_ref), custom_call_target="tpu_custom_call" | custom-call | tf_op jit(solution)/shard_map/pallas_call | solution.py:269
  65.0 3.7 %shard_map.47 = bf16[2,4,512,1024]{3,2,1,0:T(8,128)(2,1)} custom-call(bf16[4,8,256,128]{3,2,1,0:T(8,128)(2,1)S(1)} %get-tuple-element.7.d_ref, bf16[4,512,256]{2,1,0:T(8,128)(2,1)S(1)} %get-tuple-element.8.s_ref), custom_call_target="tpu_custom_call" | custom-call | tf_op jit(solution)/shard_map/pallas_call | solution.py:295

commit v4 on v3

--- a/solution.py
+++ b/solution.py
@@ -41,24 +41,19 @@
 
 def me_at():
     ch, t = lax.axis_index("chan"), lax.axis_index("tm")
-    return ch // 8, (ch // 2) % 4, (t // 2) * 2 + ch % 2, t % 2
-
-
-def ids(z, x, y, c):
-    return {"chan": z * 8 + x * 2 + y % 2, "tm": (y // 2) * 2 + c}
-
-
-def linear(z, x, y, c):
-    return (z * 8 + x * 2 + y % 2) * 4 + (y // 2) * 2 + c
+    z, y_hi = lax.div(ch, 8), lax.div(t, 2)
+    x = lax.div(ch - z * 8, 2)
+    return z, x, y_hi * 2 + ch - z * 8 - x * 2, t - y_hi * 2
 
 
 def iota(shape, dim):
     return lax.broadcasted_iota(jnp.int32, shape, dim)
 
 
-def front_kernel(x_hbm, t_hbm, small_ref, d_ref, s_ref, xv, tv, tv_first, xt, plus, minus, spec, amp, inv, sendbuf, recv, pick, x_sem, t_sem, send_sem, recv_sem, here):
+def front_kernel(x_hbm, t_hbm, valid_hbm, src_hbm, d_ref, s_ref, xv, tv, tv_first, xt, plus, minus, spec, amp, inv, sendbuf, recv, pick, early, valid_ref, src_ref, x_sem, t_sem, send_sem, recv_sem, small_sem, here):
     z, x, y, c = me_at()
-    mine = linear(z, x, y, c)
+    ch, t = lax.axis_index("chan"), lax.axis_index("tm")
+    mine = ch * 4 + t
     sign = 1 - 2 * c
     far = lax.rem(z + FAR, 8)
 
@@ -72,15 +67,23 @@
 
     x_copies[0].start()
     first_copy.start()
-
-    column = [((z + i) % 8, x, y, (c + j) % 2) for i in range(8) for j in range(2) if i or j]
-    plane = [(z, (x + i) % 4, (y + j) % 4, c) for i in range(4) for j in range(4) if i or j]
+    small_copies = [pltpu.make_async_copy(valid_hbm, valid_ref, small_sem.at[0]), pltpu.make_async_copy(src_hbm, src_ref, small_sem.at[1])]
+    for copy in small_copies:
+        copy.start()
+
+    ys = [lax.rem(y + j, 4) for j in range(4)]
+    spots = [(lax.rem(ys[j], 2), lax.div(ys[j], 2) * 2 + c) for j in range(4)]
+    column = [(lax.rem(ch + 8 * i, 64), t if j == 0 else t + 1 - 2 * c) for i in range(8) for j in range(2) if i or j]
+    plane = [(z * 8 + lax.rem(x + i, 4) * 2 + spots[j][0], spots[j][1]) for i in range(4) for j in range(4) if i or j]
+
+    def greet(devices, sem):
+        for chan, tm in devices:
+            pl.semaphore_signal(sem, inc=1, device_id={"chan": chan, "tm": tm}, device_id_type=MESH)
+
     barrier = pltpu.get_barrier_semaphore()
-    for q in column + plane:
-        pl.semaphore_signal(barrier, inc=1, device_id=ids(*q), device_id_type=MESH)
+    greet(column + plane, barrier)
 
     spread = (iota((16, LANES), 1) % 16 == iota((16, LANES), 0)).astype(F32)
-    by_channel = lax.dot_general(small_ref[0:16, 0:32].astype(F32), spread, (((0,), (0,)), ((), ())), preferred_element_type=F32)
     low = iota((1, 8, LANES), 1) < 4
     band = (jnp.abs(iota((128, 256), 0) + 64 - iota((128, 256), 1)) <= HALF_SPAN).astype(BF)
     back = (iota((128, 256), 0) + iota((128, 256), 1) == NT - 22 * 128).astype(BF)
@@ -119,6 +122,7 @@
         amp[rows, :] = (power * lax.rsqrt(jnp.maximum(power, 1e-37))).astype(BF)
 
     def valid_row(h):
+        by_channel = lax.dot_general(valid_ref[...].astype(F32), spread, (((0,), (0,)), ((), ())), preferred_element_type=F32)
         mask = iota((32, LANES), 0) == h * (LANES // 16) + iota((32, LANES), 1) // 16
         return jnp.sum(jnp.where(mask, by_channel, 0.0), axis=0, keepdims=True)
 
@@ -158,14 +162,14 @@
 
     def relay():
         pl.semaphore_wait(barrier, 30)
-        for q in plane:
-            pl.semaphore_signal(here, inc=1, device_id=ids(*q), device_id_type=MESH)
+        greet(plane, here)
 
     pl.when(z >= 4)(relay)
     fold(0)
     for b in range(4):
         t_copy(b).start()
     x_copies[1].start()
+    small_copies[0].wait()
     valid = valid_row(0)
     first_copy.wait()
     block(tv_first, pl.multiple_of(far * 128 + EDGE - HALF_SPAN, 32), 128 + 2 * HALF_SPAN)
@@ -200,12 +204,13 @@
     for pair in PHASES:
         send_planes(1, [off if off == 0 else lax.rem(8 + sign * off, 8) for off in pair])
 
-    r, p = iota((128, 128), 1), iota((128, 128), 0)
-    row_perm = (p == (r % 4) * 32 + (r // 4 % 2) * 16 + r // 8).astype(BF)
+    r, p = iota((64, 64), 1), iota((64, 64), 0)
+    row_perm = (p == (r % 4) * 16 + (r // 4 % 2) * 8 + r // 8).astype(BF)
+    small_copies[1].wait()
     for i in range(8):
-        pick[i] = (iota((128, 512), 0) + i * 128 == small_ref[16:17, :]).astype(BF).T
-
-    group = iota((128, 128), 1) // 16
+        pick[i] = (iota((128, 512), 0) + i * 128 == src_ref[...]).astype(BF).T
+
+    group = iota((64, 128), 1) // 16
 
     def swap(tiles):
         for bit in (4, 2, 1):
@@ -217,21 +222,28 @@
                     tiles[i | bit] = jnp.where(high, b, pltpu.roll(a, 128 - 16 * bit, 1))
         return tiles
 
+    def ordered(h, off):
+        part = pl.ds(lax.rem(z + 8 - off, 8) * PLANE, PLANE)
+        pltpu.make_async_copy(sendbuf.at[h, pl.ds(0, PLANE)], recv.at[h, part], recv_sem.at[h, off]).wait()
+        got = recv[h, part].reshape(8, 4, 16, 128)
+        wide = jnp.concatenate([got[i].reshape(64, 128) for i in range(8)], axis=1)
+        rows = jnp.dot(row_perm, wide, preferred_element_type=F32)
+        return swap([rows[:, i * 128:i * 128 + 128] for i in range(8)])
+
+    for j, off in enumerate(ARRIVAL[-1]):
+        for i, tile in enumerate(ordered(0, off)):
+            early[j, i] = tile
+
     for offs in ARRIVAL:
         places = [lax.rem(z + 8 - off, 8) for off in offs]
         mats = []
-        for off, zs in zip(offs, places):
-            part = pl.ds(zs * PLANE, PLANE)
-            for h in range(CHUNKS):
-                pltpu.make_async_copy(sendbuf.at[h, pl.ds(0, PLANE)], recv.at[h, part], recv_sem.at[h, off]).wait()
-            got = recv[:, part].reshape(CHUNKS, 8, 4, 16, 128)
-            wide = jnp.concatenate([got[:, i].reshape(128, 128) for i in range(8)], axis=1)
-            ordered = jnp.dot(row_perm, wide, preferred_element_type=F32)
-            tiles = [t.astype(BF) for t in swap([ordered[:, i * 128:i * 128 + 128] for i in range(8)])]
+        for j, (off, zs) in enumerate(zip(offs, places)):
+            first = [early[j, i] for i in range(8)] if offs == ARRIVAL[-1] else ordered(0, off)
+            second = ordered(1, off)
             bins = []
             for f in range(BINS):
-                at = [(f * 2 + ri) * 16 for ri in range(2)]
-                bins.append(jnp.concatenate([t[r:r + 16] for r in at for t in tiles], axis=0))
+                at = [(f * 2 + ri) * 8 for ri in range(2)]
+                bins.append(jnp.concatenate([t[i][r:r + 8] for r in at for i in range(8) for t in (first, second)], axis=0).astype(BF))
                 d_ref[f, zs] = bins[f]
             mats.append(bins)
         picks = jnp.concatenate([pick[zs] for zs in places], axis=1)
@@ -262,14 +274,13 @@
 
 def body(table, traces, valid, sources):
     rows = traces.reshape(ROWS, NT)
-    small = jnp.pad(valid.T, ((0, 8), (0, 480))) + jnp.pad(sources.reshape(1, 512), ((16, 7), (0, 0)))
     any_spec = pl.BlockSpec(memory_space=pl.ANY)
     vmem = pl.BlockSpec(memory_space=pltpu.VMEM)
     hbm = pl.BlockSpec(memory_space=pltpu.HBM)
     d, s = pl.pallas_call(
         front_kernel,
-        out_shape=(jax.ShapeDtypeStruct((BINS, 8, 256, 128), BF), jax.ShapeDtypeStruct((BINS, 512, 256), BF)),
-        in_specs=[hbm, hbm, vmem],
+        out_shape=(pltpu.VMEM((BINS, 8, 256, 128), BF), pltpu.VMEM((BINS, 512, 256), BF)),
+        in_specs=[hbm, hbm, hbm, hbm],
         out_specs=(vmem, vmem),
         scratch_shapes=[
             pltpu.VMEM((ROWS, NT), BF),
@@ -284,14 +295,18 @@
             pltpu.VMEM((CHUNKS, DEVS, 16, 128), BF),
             pltpu.VMEM((CHUNKS, DEVS, 16, 128), BF),
             pltpu.VMEM((8, 512, 128), BF),
+            pltpu.VMEM((2, 8, 64, 128), F32),
+            pltpu.VMEM((16, 32), jnp.int32),
+            pltpu.VMEM((1, 512), jnp.int32),
             pltpu.SemaphoreType.DMA((CHUNKS,)),
             pltpu.SemaphoreType.DMA((5,)),
             pltpu.SemaphoreType.DMA((CHUNKS,)),
             pltpu.SemaphoreType.DMA((CHUNKS, 8)),
+            pltpu.SemaphoreType.DMA((2,)),
             pltpu.SemaphoreType.REGULAR,
         ],
-        compiler_params=pltpu.CompilerParams(collective_id=0, has_side_effects=True, vmem_limit_bytes=48 * 2**20),
-    )(rows, table, small)
+        compiler_params=pltpu.CompilerParams(collective_id=0, has_side_effects=True, vmem_limit_bytes=52 * 2**20),
+    )(rows, table, valid.T, sources.reshape(1, 512))
     return pl.pallas_call(
         cross_kernel,
         out_shape=jax.ShapeDtypeStruct((2, BINS, 512, 1024), BF),

time: 69 us -> 68.2 us (0.988)
  other arithmetic: 0.72 us -> 0 us
    add x1 -> x0, other arithmetic: 0.72 us -> none  [body(): jnp.pad(valid.T, ((0, 8), (0, 480)))]
where the time goes in v4:
time: 68.2 us; the launch traced here: 68.1 us
  Pallas kernels  68.1 us (100%)
    pallas_call x1, Pallas kernels, body(): pl.pallas_call(front_kernel, out_shape=(pltpu.VMEM((BINS, 8, 256, 128), B...  64.4 us
    pallas_call x1, Pallas kernels, body(): pl.pallas_call(cross_kernel, out_shape=jax.ShapeDtypeStruct((2, BINS, 512...  3.72 us

profile of v4, /device:TPU:1, one launch (start us, length us, event | category | flops | bytes accessed | tf_op | source)
XLA Modules:
  0.0 68.1 jit_solution(4156644633489787325)
XLA Ops:
  0.0 64.4 %shard_map.46 = (bf16[4,8,256,128]{3,2,1,0:T(8,128)(2,1)S(1)}, bf16[4,512,256]{2,1,0:T(8,128)(2,1)S(1)}) custom-call(bf16[512,3000]{1,0:T(8,128)(2,1)} %bitcast.3, bf16[2,1152,1536]{2,1,0:T(8,128)(2,1)} %constant.2.clone.t_hbm, s32[16,32]{1,0:T(8,128)} %bitcast.4, s32[1,512]{1,0:T(1,128)} %bitcast.5), custom_call_target="tpu_custom_call" | custom-call | tf_op jit(solution)/shard_map/pallas_call | solution.py:280
  64.4 3.7 %shard_map.47 = bf16[2,4,512,1024]{3,2,1,0:T(8,128)(2,1)} custom-call(bf16[4,8,256,128]{3,2,1,0:T(8,128)(2,1)S(1)} %get-tuple-element.7.d_ref, bf16[4,512,256]{2,1,0:T(8,128)(2,1)S(1)} %get-tuple-element.8.s_ref), custom_call_target="tpu_custom_call" | custom-call | tf_op jit(solution)/shard_map/pallas_call | solution.py:310

commit v5 on v4

--- a/solution.py
+++ b/solution.py
@@ -164,7 +164,7 @@
         pl.semaphore_wait(barrier, 30)
         greet(plane, here)
 
-    pl.when(z >= 4)(relay)
+    relay()
     fold(0)
     for b in range(4):
         t_copy(b).start()
@@ -174,7 +174,6 @@
     first_copy.wait()
     block(tv_first, pl.multiple_of(far * 128 + EDGE - HALF_SPAN, 32), 128 + 2 * HALF_SPAN)
     whiten(0, far, valid)
-    pl.when(z < 4)(relay)
     pl.semaphore_wait(here, 15)
     send_planes(0, (FAR,))
 

time: 68.2 us -> 68.7 us (level)
  no operation moved by 1% of the time
where the time goes in v5:
time: 68.7 us; the launch traced here: 68.6 us
  Pallas kernels  68.6 us (100%)
    pallas_call x1, Pallas kernels, body(): pl.pallas_call(front_kernel, out_shape=(pltpu.VMEM((BINS, 8, 256, 128), B...  64.9 us
    pallas_call x1, Pallas kernels, body(): pl.pallas_call(cross_kernel, out_shape=jax.ShapeDtypeStruct((2, BINS, 512...  3.72 us

profile of v5, /device:TPU:1, one launch (start us, length us, event | category | flops | bytes accessed | tf_op | source)
XLA Modules:
  0.0 68.6 jit_solution(6778078503844621360)
XLA Ops:
  0.0 64.9 %shard_map.46 = (bf16[4,8,256,128]{3,2,1,0:T(8,128)(2,1)S(1)}, bf16[4,512,256]{2,1,0:T(8,128)(2,1)S(1)}) custom-call(bf16[512,3000]{1,0:T(8,128)(2,1)} %bitcast.3, bf16[2,1152,1536]{2,1,0:T(8,128)(2,1)} %constant.2.clone.t_hbm, s32[16,32]{1,0:T(8,128)} %bitcast.4, s32[1,512]{1,0:T(1,128)} %bitcast.5), custom_call_target="tpu_custom_call" | custom-call | tf_op jit(solution)/shard_map/pallas_call | solution.py:279
  64.9 3.7 %shard_map.47 = bf16[2,4,512,1024]{3,2,1,0:T(8,128)(2,1)} custom-call(bf16[4,8,256,128]{3,2,1,0:T(8,128)(2,1)S(1)} %get-tuple-element.7.d_ref, bf16[4,512,256]{2,1,0:T(8,128)(2,1)S(1)} %get-tuple-element.8.s_ref), custom_call_target="tpu_custom_call" | custom-call | tf_op jit(solution)/shard_map/pallas_call | solution.py:309
